TPU v7x, 32 devices: a whole 2x2x4 slice. The times are simulated.
32 devices in a mesh: dp: 4 (over z), proto: 8 (over y, x, core).
Axes of the slice: x: 2, y: 2, z: 4, core: 2. Of those that a mesh axis runs over, the one named last changes fastest.
Arguments:
- embeddings: bfloat16 [8192, 2560], P('proto', 'dp'), may hold values from -26 to 26
- table: bfloat16 [32768, 2560], P('proto', 'dp'), may hold values from -5 to 5
- tile_lists: int32 [8, 8], replicated, may hold values from 0 to 255, as said below
- labels: int32 [8192], P('proto'), may hold values from 0 to 32767, as said below
Outputs:
- loss: float32 [], replicated
- grad_emb: bfloat16 [8192, 2560], P('proto', 'dp')
- grad_table: bfloat16 [32768, 2560], P('proto', 'dp')
Inputs may be any that keep to these rules, and one draw needn't show every extreme that they name: `tile_lists`: each block's 8 tile ids are distinct and fall on exactly 4 owners (owner = id // 32), each of those owners holding exactly 2 of them. `labels`: the tile of each row's label (label // 128) is in the list of the row's block.
All inputs are finite; a program needn't handle non-finite values.
Results may differ from a plain program's by a relative error of at most 0.0025.
The roundings to bfloat16 on the way count: a program that leaves them out, or rounds other values in their place, can miss the bound.
Values may be sent and summed in bfloat16 or wider, within the bound.
A program may use at most 128 MiB of HBM per device.

v0:
```python
import math
import jax
import jax.numpy as jnp
from jax import lax
from jax.sharding import PartitionSpec as P

D = 2560
TILE = 128
CAP = 2


def slot_plan(ids, tiles_here):
    owners = ids // tiles_here
    local = ids % tiles_here
    count = ids.shape[-1]
    before = jnp.arange(count)[:, None] > jnp.arange(count)[None, :]
    earlier = (owners[..., :, None] == owners[..., None, :]) & before
    rank = jnp.sum(earlier.astype(jnp.int32), axis=-1)
    return (owners, local, rank)


def softmax_terms(scores, ids, lab, list_len):
    hit = (ids[None, :] == (lab // TILE)[:, None]).astype(jnp.int32)
    column = (
        jnp.sum(hit * (jnp.arange(list_len, dtype=jnp.int32) * TILE)[None, :], axis=1) + lab % TILE
    )
    onehot = (jnp.arange(list_len * TILE, dtype=jnp.int32)[None, :] == column[:, None]).astype(
        jnp.float32
    )
    top = jnp.max(scores, axis=1, keepdims=True)
    expo = jnp.exp(scores - top)
    total = jnp.sum(expo, axis=1, keepdims=True)
    lse = top[:, 0] + jnp.log(total[:, 0])
    target = jnp.sum(scores * onehot, axis=1)
    dz_rows = (expo / total - onehot).astype(jnp.bfloat16)
    return (jnp.sum(lse - target), dz_rows)


def body(embeddings, table, tile_lists, labels):
    block_rows, width = embeddings.shape
    list_len = tile_lists.shape[1]
    tiles_here = table.shape[0] // TILE
    groups = lax.axis_size("proto")
    dp_count = lax.axis_size("dp")
    rows_dev = block_rows // dp_count
    total_rows = block_rows * groups
    me = lax.axis_index("proto")
    part = lax.axis_index("dp")
    inv_scale = 1.0 / math.sqrt(D)
    owners, local, rank = slot_plan(tile_lists, tiles_here)
    match = (owners == me)[:, :, None] & (
        rank[:, :, None] == jnp.arange(CAP, dtype=jnp.int32)[None, None, :]
    )
    select = jnp.sum(match.astype(jnp.int32) * local[:, :, None], axis=1)
    shaped_table = table.reshape(tiles_here, TILE, width)
    outgoing = jnp.take(shaped_table, select.reshape(-1), axis=0).reshape(groups, CAP, TILE, width)
    incoming = lax.all_to_all(outgoing, "proto", split_axis=0, concat_axis=0, tiled=True)
    my_ids = lax.dynamic_index_in_dim(tile_lists, me, 0, keepdims=False)
    my_owner = lax.dynamic_index_in_dim(owners, me, 0, keepdims=False)
    my_rank = lax.dynamic_index_in_dim(rank, me, 0, keepdims=False)
    flat_slot = my_owner * CAP + my_rank
    tiles = jnp.take(incoming.reshape(groups * CAP, TILE, width), flat_slot, axis=0).reshape(
        list_len * TILE, width
    )
    scores = (
        lax.psum_scatter(
            lax.dot_general(
                embeddings, tiles, (((1,), (1,)), ((), ())), preferred_element_type=jnp.float32
            ),
            "dp",
            scatter_dimension=0,
            tiled=True,
        )
        * inv_scale
    )
    my_labels = lax.dynamic_slice_in_dim(labels, part * rows_dev, rows_dev, 0)
    loss_part, dz_rows = softmax_terms(scores, my_ids, my_labels, list_len)
    dz_block = lax.all_gather(dz_rows, "dp", axis=0, tiled=True)
    loss = lax.psum(loss_part, ("dp", "proto")) / total_rows
    grad_emb = jnp.dot(dz_block, tiles, preferred_element_type=jnp.float32).astype(jnp.bfloat16)
    piece = lax.dot_general(
        dz_block, embeddings, (((0,), (0,)), ((), ())), preferred_element_type=jnp.float32
    ).astype(jnp.bfloat16)
    returning = (
        jnp.zeros((groups * CAP, TILE, width), jnp.bfloat16)
        .at[flat_slot]
        .set(piece.reshape(list_len, TILE, width))
    )
    returned = lax.all_to_all(
        returning.reshape(groups, CAP, TILE, width),
        "proto",
        split_axis=0,
        concat_axis=0,
        tiled=True,
    )
    accum = (
        jnp.zeros((tiles_here, TILE, width), jnp.float32)
        .at[select.reshape(-1)]
        .add(returned.reshape(groups * CAP, TILE, width))
    )
    grad_table = accum.reshape(tiles_here * TILE, width).astype(jnp.bfloat16)
    return (loss, grad_emb, grad_table)


def solution(mesh):
    placed = (P("proto", "dp"), P("proto", "dp"), P(), P("proto"))
    return jax.shard_map(
        body,
        mesh=mesh,
        in_specs=placed,
        out_specs=(P(), P("proto", "dp"), P("proto", "dp")),
        check_vma=False,
    )
```

profile of v0, /device:TPU:0, one launch (start us, length us, event | category | flops | bytes accessed | tf_op | source)
XLA Modules:
  0.0 308.0 jit_solution(9859530231807013274)
XLA Ops:
  7.2 0.0 copy-start
  7.2 0.8 add_select_fusion
  8.0 0.7 broadcast_compare_fusion
  8.7 0.3 convert_reduce_fusion
  9.0 0.2 select_reduce_fusion.2
  9.1 0.1 copy.8
  9.2 0.1 copy.7
  9.3 0.1 reshape.136
  9.4 4.8 %gather_fusion = bf16[16,128,640]{2,1,0:T(8,128)(2,1)} fusion(bf16[32,128,640]{2,1,0:T(8,128)(2,1)} %bitcast.36, s32[1024]{0:T(1024)S(1)} %pad_clamp_fusion.1), kind=kCustom, calls=%fused_computation | custom fusion | bytes 5242944 | tf_op jit(solution)/shard_map/jit(_take)/gather | solution.py:56
  14.3 3.6 %broadcast_select_fusion = bf16[8,2,128,640]{3,2,1,0:T(8,128)(2,1)} fusion(bf16[8,2,128,640]{3,2,1,0:T(8,128)(2,1)} %bitcast.33, pred[8,2]{1,0:T(8,128)(4,1)S(1)} %copy.7), kind=kLoop, calls=%fused_computation.5 | loop fusion | flops 1310720 | bytes 5242896 | tf_op jit(solution)/shard_map/jit(_take)/select_n | solution.py:56
  17.8 5.2 %all-to-all-start = ((bf16[8,2,128,640]{3,2,1,0:T(8,128)(2,1)}), bf16[8,2,128,640]{3,2,1,0:T(8,128)(2,1)}, u32[]{:S(2)}, u32[]{:S(2)}) async-start(bf16[8,2,128,640]{3,2,1,0:T(8,128)(2,1)} %broadcast_select_fusion), calls=%async_computation | async-start | bytes 5242880 | tf_op jit(solution)/shard_map/all_to_all | solution.py:57
  23.0 0.0 reduce-scatter.2.cloned.1.call-start
  23.1 0.1 broadcast_bitcast_fusion
  23.2 32.2 %all-to-all-done = bf16[8,2,128,640]{3,2,1,0:T(8,128)(2,1)} async-done(((bf16[8,2,128,640]{3,2,1,0:T(8,128)(2,1)}), bf16[8,2,128,640]{3,2,1,0:T(8,128)(2,1)}, u32[]{:S(2)}, u32[]{:S(2)}) %all-to-all-start) | async-done | bytes 2621472 | tf_op jit(solution)/shard_map/all_to_all | solution.py:57
  55.4 2.5 gather_fusion.1
  57.9 0.3 bitcast_select_fusion
  58.2 0.0 copy-start.2
  58.2 1.0 copy-done.2
  59.3 0.0 copy-done
  59.3 3.8 %convolution_bitcast_fusion = f32[1024,1024]{0,1:T(8,128)} fusion(bf16[1024,640]{1,0:T(8,128)(2,1)S(1)} %bitcast_select_fusion, bf16[1024,640]{1,0:T(8,128)(2,1)S(1)} %copy-done), kind=kOutput, calls=%fused_computation.6 | convolution fusion | flops 1342177280 | bytes 6815744 | tf_op jit(solution)/shard_map/dot_general | solution.py:67
  63.1 0.0 copy-start.4
  63.1 0.0 reduce-scatter.2.cloned.1.call-update
  63.2 0.0 all-gather.2.cloned.1.call-start
  63.2 0.7 fusion.7
  63.9 0.0 copy-done.4
  63.9 0.1 and_select_fusion.1
  64.0 0.1 select_reduce_fusion.1
  64.1 0.1 fusion.4
  64.2 75.9 %reduce-scatter.2.cloned.1.call-done = f32[256,1024]{0,1:T(8,128)} async-done(((f32[1024,1024]{0,1:T(8,128)}), f32[256,1024]{0,1:T(8,128)}) %reduce-scatter.2.cloned.1.call-update) | async-done | bytes 1048592 | tf_op jit(solution)/shard_map/reduce_scatter | solution.py:66
  140.1 1.5 multiply_reduce_fusion
  141.6 1.5 fusion
  143.1 0.0 copy-done.1
  143.1 1.1 subtract_convert_fusion
  144.3 0.0 all-gather.2.cloned.1.call-update
  144.3 46.9 %all-gather.2.cloned.1.call-done = bf16[1024,1024]{0,1:T(8,128)(2,1)} async-done(((bf16[256,1024]{0,1:T(8,128)(2,1)}), bf16[1024,1024]{0,1:T(8,128)(2,1)}) %all-gather.2.cloned.1.call-update) | async-done | bytes 2097168 | tf_op jit(solution)/shard_map/all_gather | solution.py:78
  191.2 3.4 %convolution_convert_fusion = bf16[1024,640]{1,0:T(8,128)(2,1)S(1)} fusion(bf16[1024,1024]{0,1:T(8,128)(2,1)} %all-gather.2.cloned.1.call-done, bf16[1024,640]{1,0:T(8,128)(2,1)S(1)} %copy-done), kind=kOutput, calls=%fused_computation.7 | convolution fusion | flops 1342832640 | bytes 4718592 | tf_op jit(solution)/shard_map/dot_general | solution.py:81
  194.6 1.8 broadcast_in_dim.55
  196.4 3.1 scatter_fusion
  199.4 4.5 %all-to-all-start.1 = ((bf16[8,2,128,640]{3,2,1,0:T(8,128)(2,1)}), bf16[8,2,128,640]{3,2,1,0:T(8,128)(2,1)}, u32[]{:S(2)}, u32[]{:S(2)}) async-start(bf16[8,2,128,640]{3,2,1,0:T(8,128)(2,1)} %bitcast.32), calls=%async_computation.2 | async-start | bytes 5242880 | tf_op jit(solution)/shard_map/all_to_all | solution.py:89
  203.9 0.6 subtract_reduce_fusion
  204.5 62.9 %psum.7 = f32[]{:T(128)} all-reduce(f32[]{:T(128)} %subtract_reduce_fusion), channel_id=1, replica_groups=mesh['dp'=4,'proto'=8] {'dp','proto'}, use_global_device_ids=true, to_apply=%region_8.9 | all-reduce | flops 1 | bytes 8 | tf_op jit(solution)/shard_map/psum | solution.py:79
  268.1 0.0 copy-done.3
  268.1 4.5 %convolution_convert_fusion.1 = bf16[1024,640]{1,0:T(8,128)(2,1)} fusion(bf16[1024,1024]{0,1:T(8,128)(2,1)} %all-gather.2.cloned.1.call-done, bf16[1024,640]{1,0:T(8,128)(2,1)S(1)} %copy-done.3), kind=kOutput, calls=%fused_computation.8 | convolution fusion | flops 1342832640 | bytes 4718592 | tf_op jit(solution)/shard_map/dot_general | solution.py:80
  272.6 0.0 all-to-all-done.1
  272.6 4.6 %bitcast_convert_fusion = f32[16,128,640]{2,1,0:T(8,128)} fusion(bf16[8,2,128,640]{3,2,1,0:T(8,128)(2,1)} %all-to-all-done.1), kind=kLoop, calls=%fused_computation.4 | loop fusion | flops 1310720 | bytes 7864320 | tf_op jit(solution)/shard_map/convert_element_type | solution.py:99
  277.3 5.2 %broadcast_in_dim.54 = f32[32,128,640]{2,1,0:T(8,128)} broadcast(f32[]{:T(128)} %constant.115.clone.1), dimensions={} | broadcast | bytes 10485764 | tf_op jit(solution)/shard_map/broadcast_in_dim | solution.py:97
  282.5 10.5 %scatter_fusion.1 = f32[32,128,640]{2,1,0:T(8,128)} fusion(f32[32,128,640]{2,1,0:T(8,128)} %broadcast_in_dim.54, s32[16]{0:T(128)S(1)} %fusion.8, f32[16,128,640]{2,1,0:T(8,128)} %bitcast_convert_fusion), kind=kCustom, calls=%fused_computation.3 | custom fusion | flops 1310720 | bytes 15728704 | tf_op jit(solution)/shard_map/scatter-add | solution.py:99
  292.9 7.1 %convert_element_type.36 = bf16[32,128,640]{2,1,0:T(8,128)(2,1)} convert(f32[32,128,640]{2,1,0:T(8,128)} %scatter_fusion.1) | non-fusion elementwise | flops 2621440 | bytes 15728640 | tf_op jit(solution)/shard_map/convert_element_type | solution.py:101
  (9 shorter events, 0.1 us)
Async XLA Ops:
  7.2 52.1 %copy-start = (bf16[1024,640]{1,0:T(8,128)(2,1)S(1)}, bf16[1024,640]{1,0:T(8,128)(2,1)}, u32[]{:S(2)}) copy-start(bf16[1024,640]{1,0:T(8,128)(2,1)} %param.4) | copy-start | bytes 3932164
  17.8 37.5 %all-to-all-start = ((bf16[8,2,128,640]{3,2,1,0:T(8,128)(2,1)}), bf16[8,2,128,640]{3,2,1,0:T(8,128)(2,1)}, u32[]{:S(2)}, u32[]{:S(2)}) async-start(bf16[8,2,128,640]{3,2,1,0:T(8,128)(2,1)} %broadcast_select_fusion), calls=%async_computation | async-start | bytes 5242880 | tf_op jit(solution)/shard_map/all_to_all | solution.py:57
  23.0 117.1 %reduce-scatter.2.cloned.1.call-start = ((), (), s32[]{:S(2)}) async-start(), calls=%async_computation.3 | async-start | bytes 5242880 | tf_op jit(solution)/shard_map/reduce_scatter | solution.py:66
  58.2 1.1 copy-start.2
  63.1 0.8 copy-start.4
  63.2 128.0 %all-gather.2.cloned.1.call-start = ((), (), s32[]{:S(2)}) async-start(), calls=%async_computation.4 | async-start | bytes 2621440 | tf_op jit(solution)/shard_map/all_gather | solution.py:78
  140.1 3.0 copy-start.1
  199.4 68.7 %copy-start.3 = (bf16[1024,640]{1,0:T(8,128)(2,1)S(1)}, bf16[1024,640]{1,0:T(8,128)(2,1)}, u32[]{:S(2)}) copy-start(bf16[1024,640]{1,0:T(8,128)(2,1)} %copy-done.2) | copy-start | bytes 3932164
  199.4 73.2 %all-to-all-start.1 = ((bf16[8,2,128,640]{3,2,1,0:T(8,128)(2,1)}), bf16[8,2,128,640]{3,2,1,0:T(8,128)(2,1)}, u32[]{:S(2)}, u32[]{:S(2)}) async-start(bf16[8,2,128,640]{3,2,1,0:T(8,128)(2,1)} %bitcast.32), calls=%async_computation.2 | async-start | bytes 5242880 | tf_op jit(solution)/shard_map/all_to_all | solution.py:89
Sparse Core Ops, SparseCore 0:
  63.3 76.7 reduce-scatter.1
  144.4 46.7 all-gather.1
where the time goes:
time: 309 us; the launch traced here: 308 us
  waiting for transfers between devices  155 us (50%)
  blocking collectives  62.9 us (20%)
  other arithmetic  33.1 us (11%)
  local copies, waits for them, and re-layouts  19.5 us (6%)
  between operations  15.9 us (5%)
  matrix products  11.7 us (4%)
  starting transfers between devices  9.76 us (3%)
    reduce_scatter x1, waiting for transfers between devices, body(): lax.psum_scatter(lax.dot_general(embeddings, tiles, (((1,), (1,)), ((), (...  75.9 us
    psum x1, blocking collectives, body(): loss = lax.psum(loss_part, ('dp', 'proto')) / total_rows  62.9 us
    all_gather x1, waiting for transfers between devices, body(): dz_block = lax.all_gather(dz_rows, 'dp', axis=0, tiled=True)  46.9 us
    all_to_all x1, waiting for transfers between devices, body(): lax.all_to_all(outgoing, 'proto', split_axis=0, concat_axis=0, tiled=True)  32.2 us
    scatter-add x1, other arithmetic, body(): accum = jnp.zeros((tiles_here, TILE, width), jnp.float32).at[select.resha...  10.5 us
    convert_element_type x1, other arithmetic, body(): grad_table = accum.reshape(tiles_here * TILE, width).astype(jnp.bfloat16)  7.1 us
  transfers between devices with their start and end apart: 4, of which 3 were waited for; matrix products, arithmetic and copies ran while one was open for 2% of the time, Pallas kernels for 0%

commit v1 on v0

--- a/solution.py
+++ b/solution.py
@@ -7,6 +7,28 @@
 D = 2560
 TILE = 128
 CAP = 2
+
+
+def joined_along(blocks, dim):
+    dims = list(blocks.shape[1:])
+    dims[dim] *= blocks.shape[0]
+    return jnp.moveaxis(blocks, 0, dim).reshape(dims)
+
+
+def gather_around(x, axis, dim):
+    size = lax.axis_size(axis)
+    pairs = [(i, (i + 1) % size) for i in range(size)]
+    back = [(b, a) for a, b in pairs]
+    lower, upper = ([], [])
+    for lap in range(size - 1):
+        if lap % 2 == 0:
+            lower.append(lax.ppermute(lower[-1] if lower else x, axis, pairs))
+        else:
+            upper.append(lax.ppermute(upper[-1] if upper else x, axis, back))
+    blocks = jnp.stack([*lower[::-1], x, *upper])
+    shift = lax.axis_index(axis) - len(lower)
+    blocks = blocks[(jnp.arange(size) - shift) % size]
+    return joined_along(blocks, dim)
 
 
 def slot_plan(ids, tiles_here):
@@ -75,7 +97,7 @@
     )
     my_labels = lax.dynamic_slice_in_dim(labels, part * rows_dev, rows_dev, 0)
     loss_part, dz_rows = softmax_terms(scores, my_ids, my_labels, list_len)
-    dz_block = lax.all_gather(dz_rows, "dp", axis=0, tiled=True)
+    dz_block = gather_around(dz_rows, "dp", 0)
     loss = lax.psum(loss_part, ("dp", "proto")) / total_rows
     grad_emb = jnp.dot(dz_block, tiles, preferred_element_type=jnp.float32).astype(jnp.bfloat16)
     piece = lax.dot_general(

time: 309 us -> 305 us (0.987)
  waiting for transfers between devices: 155 us -> 133 us
  starting transfers between devices: 9.76 us -> 22.6 us
  local copies, waits for them, and re-layouts: 19.5 us -> 23.5 us
    all_gather x1 -> x0, waiting for transfers between devices: 46.9 us -> none  [body(): dz_block = lax.all_gather(dz_rows, 'dp', axis=0, tiled=True)]
    ppermute x0 -> x3, waiting for transfers between devices: none -> 24.9 us  [the longest x2 23.7 us: gather_around(): lower.append(lax.ppermute(lower[-1] if lower else x, axis, pairs))]
    ppermute x0 -> x3, starting transfers between devices: none -> 12.9 us  [the longest x2 10.5 us: gather_around(): lower.append(lax.ppermute(lower[-1] if lower else x, axis, pairs))]
    gather x0 -> x2, local copies, waits for them, and re-layouts: none -> 4.98 us  [gather_around(): blocks = blocks[(jnp.arange(size) - shift) % size]]
  transfers between devices with their start and end apart: 4 -> 6, of which waited for: 3 -> 5; matrix products, arithmetic and copies ran while one was open for 2% -> 3% of each run, Pallas kernels for 0% -> 0%
where the time goes in v1:
time: 305 us; the launch traced here: 304 us
  waiting for transfers between devices  133 us (44%)
  blocking collectives  61.6 us (20%)
  other arithmetic  35.6 us (12%)
  local copies, waits for them, and re-layouts  23.5 us (8%)
  starting transfers between devices  22.6 us (7%)
  between operations  16 us (5%)
  matrix products  11.5 us (4%)
    reduce_scatter x1, waiting for transfers between devices, body(): lax.psum_scatter(lax.dot_general(embeddings, tiles, (((1,), (1,)), ((), (...  75.9 us
    psum x1, blocking collectives, body(): loss = lax.psum(loss_part, ('dp', 'proto')) / total_rows  61.6 us
    all_to_all x1, waiting for transfers between devices, body(): lax.all_to_all(outgoing, 'proto', split_axis=0, concat_axis=0, tiled=True)  32.2 us
    ppermute x2, waiting for transfers between devices, gather_around(): lower.append(lax.ppermute(lower[-1] if lower else x, axis, pairs))  23.7 us
    ppermute x2, starting transfers between devices, gather_around(): lower.append(lax.ppermute(lower[-1] if lower else x, axis, pairs))  10.5 us
    scatter-add x1, other arithmetic, body(): accum = jnp.zeros((tiles_here, TILE, width), jnp.float32).at[select.resha...  10.5 us
    convert_element_type x1, other arithmetic, body(): grad_table = accum.reshape(tiles_here * TILE, width).astype(jnp.bfloat16)  7.1 us
  transfers between devices with their start and end apart: 6, of which 5 were waited for; matrix products, arithmetic and copies ran while one was open for 3% of the time, Pallas kernels for 0%

profile of v1, /device:TPU:0, one launch (start us, length us, event | category | flops | bytes accessed | tf_op | source)
XLA Modules:
  0.0 303.9 jit_solution(1479294771423388499)
XLA Ops:
  7.2 0.0 copy-start
  7.2 0.8 add_select_fusion
  8.0 0.7 broadcast_compare_fusion
  8.7 0.3 convert_reduce_fusion
  9.0 0.2 select_reduce_fusion.2
  9.1 0.1 copy.9
  9.2 0.1 copy.8
  9.3 0.1 reshape.218
  9.4 4.8 %gather_fusion = bf16[16,128,640]{2,1,0:T(8,128)(2,1)} fusion(bf16[32,128,640]{2,1,0:T(8,128)(2,1)} %bitcast.47, s32[1024]{0:T(1024)S(1)} %pad_clamp_fusion.2), kind=kCustom, calls=%fused_computation | custom fusion | bytes 5242944 | tf_op jit(solution)/shard_map/jit(_take)/gather | solution.py:78
  14.3 3.6 %broadcast_select_fusion = bf16[8,2,128,640]{3,2,1,0:T(8,128)(2,1)} fusion(bf16[8,2,128,640]{3,2,1,0:T(8,128)(2,1)} %bitcast.42, pred[8,2]{1,0:T(8,128)(4,1)S(1)} %copy.8), kind=kLoop, calls=%fused_computation.6 | loop fusion | flops 1310720 | bytes 5242896 | tf_op jit(solution)/shard_map/jit(_take)/select_n | solution.py:78
  17.8 5.2 %all-to-all-start = ((bf16[8,2,128,640]{3,2,1,0:T(8,128)(2,1)}), bf16[8,2,128,640]{3,2,1,0:T(8,128)(2,1)}, u32[]{:S(2)}, u32[]{:S(2)}) async-start(bf16[8,2,128,640]{3,2,1,0:T(8,128)(2,1)} %broadcast_select_fusion), calls=%async_computation | async-start | bytes 5242880 | tf_op jit(solution)/shard_map/all_to_all | solution.py:79
  23.0 0.0 reduce-scatter.2.cloned.1.call-start
  23.1 0.1 broadcast_bitcast_fusion
  23.2 32.2 %all-to-all-done = bf16[8,2,128,640]{3,2,1,0:T(8,128)(2,1)} async-done(((bf16[8,2,128,640]{3,2,1,0:T(8,128)(2,1)}), bf16[8,2,128,640]{3,2,1,0:T(8,128)(2,1)}, u32[]{:S(2)}, u32[]{:S(2)}) %all-to-all-start) | async-done | bytes 2621472 | tf_op jit(solution)/shard_map/all_to_all | solution.py:79
  55.4 2.5 gather_fusion.1
  57.9 0.3 bitcast_select_fusion
  58.2 3.8 %convolution_bitcast_fusion = f32[1024,1024]{0,1:T(8,128)} fusion(bf16[1024,640]{1,0:T(8,128)(2,1)S(1)} %bitcast_select_fusion, bf16[1024,640]{1,0:T(8,128)(2,1)S(1)} %copy-done), kind=kOutput, calls=%fused_computation.7 | convolution fusion | flops 1342177280 | bytes 6815744 | tf_op jit(solution)/shard_map/dot_general | solution.py:89
  62.1 0.0 reduce-scatter.2.cloned.1.call-update
  62.1 0.7 fusion.7
  62.8 0.1 and_select_fusion.2
  62.9 0.1 select_reduce_fusion.1
  63.0 0.1 fusion.4
  63.1 75.9 %reduce-scatter.2.cloned.1.call-done = f32[256,1024]{0,1:T(8,128)} async-done(((f32[1024,1024]{0,1:T(8,128)}), f32[256,1024]{0,1:T(8,128)}) %reduce-scatter.2.cloned.1.call-update) | async-done | bytes 1048592 | tf_op jit(solution)/shard_map/reduce_scatter | solution.py:88
  139.0 1.5 multiply_reduce_fusion
  140.5 1.5 fusion
  142.1 0.3 subtract_convert_fusion
  142.4 1.5 collective-permute-start
  143.9 2.3 collective-permute-start.2
  146.3 12.8 %collective-permute-done = bf16[256,1024]{0,1:T(8,128)(2,1)S(1)} collective-permute-done((bf16[256,1024]{0,1:T(8,128)(2,1)S(1)}, bf16[256,1024]{0,1:T(8,128)(2,1)S(1)}, u32[]{:S(2)}, u32[]{:S(2)}) %collective-permute-start) | collective-permute-done | bytes 524320 | tf_op jit(solution)/shard_map/ppermute | solution.py:25
  159.1 9.0 %collective-permute-start.1 = (bf16[256,1024]{0,1:T(8,128)(2,1)S(1)}, bf16[256,1024]{0,1:T(8,128)(2,1)}, u32[]{:S(2)}, u32[]{:S(2)}) collective-permute-start(bf16[256,1024]{0,1:T(8,128)(2,1)S(1)} %collective-permute-done), channel_id=1, source_target_pairs={{0,8},{8,16},{16,24},{24,0},{1,9},{9,17},{17,25},{25,1},{2,10},{10... | collective-permute-start | bytes 1572872 | tf_op jit(solution)/shard_map/ppermute | solution.py:25
  168.1 0.3 fusion.19
  168.5 1.3 collective-permute-done.2
  169.7 10.9 %collective-permute-done.1 = bf16[256,1024]{0,1:T(8,128)(2,1)} collective-permute-done((bf16[256,1024]{0,1:T(8,128)(2,1)S(1)}, bf16[256,1024]{0,1:T(8,128)(2,1)}, u32[]{:S(2)}, u32[]{:S(2)}) %collective-permute-start.1) | collective-permute-done | bytes 524320 | tf_op jit(solution)/shard_map/ppermute | solution.py:25
  180.6 1.6 pad_maximum_fusion
  182.2 2.0 gather_fusion.2
  184.2 3.0 copy.10
  187.2 2.9 convolution_convert_fusion
  190.1 1.8 broadcast_in_dim.62
  191.9 3.1 %scatter_fusion = bf16[16,128,640]{2,1,0:T(8,128)(2,1)} fusion(bf16[16,128,640]{2,1,0:T(8,128)(2,1)} %broadcast_in_dim.62, s32[8]{0:T(128)S(1)} %fusion.10, bf16[8,128,640]{2,1,0:T(8,128)(2,1)S(1)} %bitcast.46), kind=kCustom, calls=%fused_computation.3 | custom fusion | bytes 3932192 | tf_op jit(solution)/shard_map/scatter | solution.py:109
  195.0 4.5 %all-to-all-start.1 = ((bf16[8,2,128,640]{3,2,1,0:T(8,128)(2,1)}), bf16[8,2,128,640]{3,2,1,0:T(8,128)(2,1)}, u32[]{:S(2)}, u32[]{:S(2)}) async-start(bf16[8,2,128,640]{3,2,1,0:T(8,128)(2,1)} %bitcast.41), calls=%async_computation.2 | async-start | bytes 5242880 | tf_op jit(solution)/shard_map/all_to_all | solution.py:111
  199.5 0.6 subtract_reduce_fusion
  200.1 1.3 broadcast_select_fusion.1
  201.4 61.6 %psum.7 = f32[]{:T(128)} all-reduce(f32[]{:T(128)} %subtract_reduce_fusion), channel_id=1, replica_groups=mesh['dp'=4,'proto'=8] {'dp','proto'}, use_global_device_ids=true, to_apply=%region_8.9 | all-reduce | flops 1 | bytes 8 | tf_op jit(solution)/shard_map/psum | solution.py:101
  263.7 4.8 %convolution_convert_fusion.1 = bf16[1024,640]{1,0:T(8,128)(2,1)} fusion(bf16[1024,1024]{1,0:T(8,128)(2,1)} %bitcast.45, bf16[1024,640]{1,0:T(8,128)(2,1)} %bitcast.48), kind=kOutput, calls=%fused_computation.10 | convolution fusion | flops 1342832640 | bytes 4718592 | tf_op jit(solution)/shard_map/dot_general | solution.py:102
  268.5 4.6 %bitcast_convert_fusion = f32[16,128,640]{2,1,0:T(8,128)} fusion(bf16[8,2,128,640]{3,2,1,0:T(8,128)(2,1)} %all-to-all-done.1), kind=kLoop, calls=%fused_computation.5 | loop fusion | flops 1310720 | bytes 7864320 | tf_op jit(solution)/shard_map/convert_element_type | solution.py:121
  273.1 5.2 %broadcast_in_dim.61 = f32[32,128,640]{2,1,0:T(8,128)} broadcast(f32[]{:T(128)} %constant.131.clone.1), dimensions={} | broadcast | bytes 10485764 | tf_op jit(solution)/shard_map/broadcast_in_dim | solution.py:119
  278.3 10.5 %scatter_fusion.1 = f32[32,128,640]{2,1,0:T(8,128)} fusion(f32[32,128,640]{2,1,0:T(8,128)} %broadcast_in_dim.61, s32[16]{0:T(128)S(1)} %fusion.9, f32[16,128,640]{2,1,0:T(8,128)} %bitcast_convert_fusion), kind=kCustom, calls=%fused_computation.4 | custom fusion | flops 1310720 | bytes 15728704 | tf_op jit(solution)/shard_map/scatter-add | solution.py:121
  288.8 7.1 %convert_element_type.36 = bf16[32,128,640]{2,1,0:T(8,128)(2,1)} convert(f32[32,128,640]{2,1,0:T(8,128)} %scatter_fusion.1) | non-fusion elementwise | flops 2621440 | bytes 15728640 | tf_op jit(solution)/shard_map/convert_element_type | solution.py:123
  (25 shorter events, 0.1 us)
Async XLA Ops:
  7.2 51.1 %copy-start = (bf16[1024,640]{1,0:T(8,128)(2,1)S(1)}, bf16[1024,640]{1,0:T(8,128)(2,1)}, u32[]{:S(2)}) copy-start(bf16[1024,640]{1,0:T(8,128)(2,1)} %param.4) | copy-start | bytes 3932164
  17.8 37.5 %all-to-all-start = ((bf16[8,2,128,640]{3,2,1,0:T(8,128)(2,1)}), bf16[8,2,128,640]{3,2,1,0:T(8,128)(2,1)}, u32[]{:S(2)}, u32[]{:S(2)}) async-start(bf16[8,2,128,640]{3,2,1,0:T(8,128)(2,1)} %broadcast_select_fusion), calls=%async_computation | async-start | bytes 5242880 | tf_op jit(solution)/shard_map/all_to_all | solution.py:79
  23.0 116.0 %reduce-scatter.2.cloned.1.call-start = ((), (), s32[]{:S(2)}) async-start(), calls=%async_computation.3 | async-start | bytes 5242880 | tf_op jit(solution)/shard_map/reduce_scatter | solution.py:88
  57.9 4.2 %copy-start.2 = (bf16[8,128,640]{2,1,0:T(8,128)(2,1)}, bf16[8,128,640]{2,1,0:T(8,128)(2,1)S(1)}, u32[]{:S(2)}) copy-start(bf16[8,128,640]{2,1,0:T(8,128)(2,1)S(1)} %gather_fusion.1) | copy-start | bytes 3932164
  62.1 0.7 copy-start.7
  139.0 3.0 copy-start.1
  142.4 16.7 %collective-permute-start = (bf16[256,1024]{0,1:T(8,128)(2,1)S(1)}, bf16[256,1024]{0,1:T(8,128)(2,1)S(1)}, u32[]{:S(2)}, u32[]{:S(2)}) collective-permute-start(bf16[256,1024]{0,1:T(8,128)(2,1)S(1)} %subtract_convert_fusion), channel_id=1, source_target_pairs={{0,8},{8,16},{16,24},{24,0},{1,9},{9,17},{17,25},{25,1},{2,10},{10... | collective-permute-start | bytes 1572872 | tf_op jit(solution)/shard_map/ppermute | solution.py:25
  143.9 25.8 %collective-permute-start.2 = (bf16[256,1024]{0,1:T(8,128)(2,1)S(1)}, bf16[256,1024]{0,1:T(8,128)(2,1)}, u32[]{:S(2)}, u32[]{:S(2)}) collective-permute-start(bf16[256,1024]{0,1:T(8,128)(2,1)S(1)} %subtract_convert_fusion), channel_id=1, source_target_pairs={{8,0},{16,8},{24,16},{0,24},{9,1},{17,9},{25,17},{1,25},{10,2},{18... | collective-permute-start | bytes 1572872 | tf_op jit(solution)/shard_map/ppermute | solution.py:27
  159.1 21.5 %copy-start.6 = (bf16[256,1024]{0,1:T(8,128)(2,1)}, bf16[256,1024]{0,1:T(8,128)(2,1)S(1)}, u32[]{:S(2)}) copy-start(bf16[256,1024]{0,1:T(8,128)(2,1)S(1)} %collective-permute-done) | copy-start | bytes 1572868
  159.1 21.5 %collective-permute-start.1 = (bf16[256,1024]{0,1:T(8,128)(2,1)S(1)}, bf16[256,1024]{0,1:T(8,128)(2,1)}, u32[]{:S(2)}, u32[]{:S(2)}) collective-permute-start(bf16[256,1024]{0,1:T(8,128)(2,1)S(1)} %collective-permute-done), channel_id=1, source_target_pairs={{0,8},{8,16},{16,24},{24,0},{1,9},{9,17},{17,25},{25,1},{2,10},{10... | collective-permute-start | bytes 1572872 | tf_op jit(solution)/shard_map/ppermute | solution.py:25
  187.2 2.9 copy-start.4
  190.1 1.8 copy-start.5
  195.0 5.1 %copy-start.3 = (bf16[8,128,640]{2,1,0:T(8,128)(2,1)S(1)}, bf16[8,128,640]{2,1,0:T(8,128)(2,1)}, u32[]{:S(2)}) copy-start(bf16[8,128,640]{2,1,0:T(8,128)(2,1)} %copy-done.2) | copy-start | bytes 3932164
  195.0 73.5 %all-to-all-start.1 = ((bf16[8,2,128,640]{3,2,1,0:T(8,128)(2,1)}), bf16[8,2,128,640]{3,2,1,0:T(8,128)(2,1)}, u32[]{:S(2)}, u32[]{:S(2)}) async-start(bf16[8,2,128,640]{3,2,1,0:T(8,128)(2,1)} %bitcast.41), calls=%async_computation.2 | async-start | bytes 5242880 | tf_op jit(solution)/shard_map/all_to_all | solution.py:111
Sparse Core Ops, SparseCore 0:
  62.2 76.7 reduce-scatter.1
